TPU v7x, 32 devices: a whole 2x2x4 slice. The times are simulated.
32 devices in a mesh: grp: 2 (over x), tm: 16 (over z, y, core).
Axes of the slice: x: 2, y: 2, z: 4, core: 2. Of those that a mesh axis runs over, the one named last changes fastest.
Arguments:
- series: bfloat16 [3072, 49152], P('tm', 'grp'), parts along dimension 1, may hold values from -6 to 6
- filter_taps: bfloat16 [201], replicated, may hold values from -0.4375 to 0.4375
- test_matrix: bfloat16 [24576, 128], replicated, may hold values from -0.0390625 to 0.0390625
Outputs:
- patterns: float32 [49152, 128], P(('grp', 'tm')), parts along dimension 0
- factor: float32 [256, 128], P('grp'), parts along dimension 0
There are 2 independent parts, one for each index of `grp`. A program takes and returns all parts, laid end to end along the dimension named above; an argument that names none is the same for every part. Nothing has to cross between parts.
All inputs are finite; a program needn't handle non-finite values.
Results may differ from a plain program's by a relative error of at most 0.0006.
The roundings to bfloat16 on the way count: a program that leaves them out, or rounds other values in their place, can miss the bound.
Values may be sent and summed in bfloat16 or wider, within the bound.
A program may use at most 128 MiB of HBM per device.

v0:
```python
import jax
import jax.numpy as jnp
from jax import lax
from jax.sharding import PartitionSpec as P


def with_halo(cells, sides, width):
    for axis, dim in sides:
        count = lax.axis_size(axis)
        ends = count - 1
        head = lax.slice_in_dim(cells, 0, width, axis=dim)
        tail = lax.slice_in_dim(cells, cells.shape[dim] - width, cells.shape[dim], axis=dim)
        cells = jnp.concatenate(
            [
                lax.ppermute(tail, axis, [(i, (i + 1) % count) for i in range(ends)]),
                cells,
                lax.ppermute(head, axis, [((i + 1) % count, i) for i in range(ends)]),
            ],
            axis=dim,
        )
    return cells


def toeplitz_rows(filter_taps, day_count):
    width = filter_taps.shape[0]
    row_len = width + day_count
    padded_taps = jnp.concatenate([filter_taps, jnp.zeros((day_count,), filter_taps.dtype)])
    flat = jnp.tile(padded_taps, day_count)[: day_count * (row_len - 1)]
    return flat.reshape(day_count, row_len - 1)


def on_device(series, filter_taps, test_matrix):
    day_count = series.shape[0]
    half_width = (filter_taps.shape[0] - 1) // 2
    padded = with_halo(series, (("tm", 0),), half_width)
    toeplitz = toeplitz_rows(filter_taps, day_count)
    filtered = jnp.dot(toeplitz, padded, preferred_element_type=jnp.float32).astype(jnp.bfloat16)
    sketch = jnp.dot(filtered, test_matrix, preferred_element_type=jnp.float32).astype(jnp.bfloat16)
    local_gram = jnp.einsum("tr,ts->rs", sketch, sketch, preferred_element_type=jnp.float32)
    gram_sum = lax.psum(local_gram, "tm")
    lower_factor = jnp.linalg.cholesky(gram_sum)
    cross_sums = lax.psum_scatter(
        jnp.einsum("tc,tr->cr", filtered, sketch, preferred_element_type=jnp.float32),
        "tm",
        scatter_dimension=0,
        tiled=True,
    )
    patterns = lax.linalg.triangular_solve(
        lower_factor, cross_sums, left_side=False, lower=True, transpose_a=True
    )
    total_days = day_count * lax.axis_size("tm")
    factor = lower_factor.T * float(total_days) ** (-0.5)
    return (patterns, factor)


def solution(mesh):
    placed = (P("tm", "grp"), P(), P())
    return jax.shard_map(
        on_device,
        mesh=mesh,
        in_specs=placed,
        out_specs=(P(("grp", "tm"), None), P("grp", None)),
        check_vma=False,
    )
```

profile of v0, /device:TPU:8, one launch (start us, length us, event | category | flops | bytes accessed | tf_op | source)
XLA Modules:
  0.0 387.1 jit_solution(15878972797090855388)
XLA Ops:
  7.2 0.0 all-reduce.3.cloned.1.call-start
  7.2 9.1 %fusion.9 = (bf16[100,24576]{1,0:T(8,128)(2,1)}, bf16[100,24576]{1,0:T(8,128)(2,1)}) fusion(bf16[192,24576]{1,0:T(8,128)(2,1)} %param.3), kind=kLoop, calls=%fused_computation.19 | loop fusion | bytes 19660800 | tf_op jit(solution)/shard_map/slice | solution.py:12
  16.3 2.7 collective-permute-start.1
  19.0 1.9 collective-permute-start
  21.0 0.4 tile.10
  21.4 0.4 reshape.17
  21.8 53.4 %collective-permute-done.1 = bf16[100,24576]{1,0:T(8,128)(2,1)} collective-permute-done((bf16[100,24576]{1,0:T(8,128)(2,1)}, bf16[100,24576]{1,0:T(8,128)(2,1)}, u32[]{:S(2)}, u32[]{:S(2)}) %collective-permute-start.1) | collective-permute-done | bytes 4915232 | tf_op jit(solution)/shard_map/ppermute | solution.py:17
  75.2 4.8 %collective-permute-done = bf16[100,24576]{1,0:T(8,128)(2,1)} collective-permute-done((bf16[100,24576]{1,0:T(8,128)(2,1)}, bf16[100,24576]{1,0:T(8,128)(2,1)}, u32[]{:S(2)}, u32[]{:S(2)}) %collective-permute-start) | collective-permute-done | bytes 4915232 | tf_op jit(solution)/shard_map/ppermute | solution.py:15
  80.0 10.6 %convolution_convert_fusion = bf16[192,24576]{1,0:T(8,128)(2,1)S(1)} fusion(bf16[192,392]{1,0:T(8,128)(2,1)S(1)} %reshape.17, bf16[100,24576]{1,0:T(8,128)(2,1)} %collective-permute-done.1, bf16[192,24576]{1,0:T(8,128)(2,1)} %param.3, bf16[100,24576]{1,0:T(8,128)(2,1)} %collective-permute-done), kind=kOutput, calls=%fused_computation | convolution fusion | flops 3761897472 | bytes 28855296 | tf_op jit(solution)/shard_map/dot_general | solution.py:37
  90.6 8.9 %convolution_convert_fusion.1 = bf16[192,128]{1,0:T(8,128)(2,1)S(1)} fusion(bf16[192,24576]{1,0:T(8,128)(2,1)S(1)} %convolution_convert_fusion, bf16[24576,128]{1,0:T(8,128)(2,1)} %param.5), kind=kOutput, calls=%fused_computation.6 | convolution fusion | flops 1207984128 | bytes 15777792 | tf_op jit(solution)/shard_map/dot_general | solution.py:38
  99.5 0.8 fusion.11
  100.4 0.2 reduce-scatter.2.cloned.1.call-start
  100.6 11.8 %fusion.10 = f32[24576,128]{1,0:T(8,128)} fusion(bf16[192,24576]{1,0:T(8,128)(2,1)} %copy-done, bf16[192,128]{1,0:T(8,128)(2,1)S(1)} %convolution_convert_fusion.1), kind=kOutput, calls=%fused_computation.20 | convolution fusion | flops 1207959552 | bytes 22069248 | tf_op jit(solution)/shard_map/tc,tr->cr/dot_general | solution.py:43
  112.4 0.0 reduce-scatter.2.cloned.1.call-update
  112.5 127.2 %all-reduce.3.cloned.1.call-done = f32[128,128]{0,1:T(8,128)} async-done(((f32[128,128]{0,1:T(8,128)}), f32[128,128]{0,1:T(8,128)}) %all-reduce.3.cloned.1.call-update) | async-done | bytes 65552 | tf_op jit(solution)/shard_map/psum | solution.py:40
  239.7 0.9 copy.6
  240.6 0.9 fusion.7
  241.4 11.7 %cholesky.16 = f32[128,128]{1,0:T(8,128)S(1)} custom-call(f32[128,128]{1,0:T(8,128)S(1)} %fusion.7), custom_call_target="Cholesky" | custom-call | tf_op jit(solution)/shard_map/jit(cholesky)/cholesky | solution.py:41
  253.2 0.6 compare_reduce_fusion
  253.8 0.7 multiply_bitcast_fusion
  254.5 9.8 %custom-call.6 = f32[1,128,128]{1,2,0:T(8,128)S(1)} custom-call(f32[1,128,128]{2,1,0:T(8,128)S(1)} %get-tuple-element.7), custom_call_target="InvertDiagBlocksLowerTriangular" | custom-call | tf_op jit(solution)/shard_map/triangular_solve | solution.py:48
  264.3 0.7 copy.7
  265.1 112.4 %reduce-scatter.2.cloned.1.call-done = f32[1536,128]{1,0:T(8,128)} async-done(((f32[24576,128]{1,0:T(8,128)}), f32[1536,128]{1,0:T(8,128)}) %reduce-scatter.2.cloned.1.call-update) | async-done | bytes 786448 | tf_op jit(solution)/shard_map/reduce_scatter | solution.py:42
  377.5 2.8 fusion.5
  (8 shorter events, 0.1 us)
Async XLA Ops:
  7.2 13.8 %copy-start.1 = (bf16[201]{0:T(256)(128)(2,1)S(1)}, bf16[201]{0:T(256)(128)(2,1)}, u32[]{:S(2)}) copy-start(bf16[201]{0:T(256)(128)(2,1)} %param.4) | copy-start | bytes 1210
  7.2 232.5 %all-reduce.3.cloned.1.call-start = ((), (), s32[]{:S(2)}) async-start(), calls=%async_computation.2 | async-start | bytes 131072 | tf_op jit(solution)/shard_map/psum | solution.py:40
  16.3 58.9 %collective-permute-start.1 = (bf16[100,24576]{1,0:T(8,128)(2,1)}, bf16[100,24576]{1,0:T(8,128)(2,1)}, u32[]{:S(2)}, u32[]{:S(2)}) collective-permute-start(bf16[100,24576]{1,0:T(8,128)(2,1)} %get-tuple-element.5), channel_id=1, source_target_pairs={{1,0},{2,1},{3,2},{4,3},{5,4},{6,5},{7,6},{8,7},{9,8},{10,9},{11,1... | collective-permute-start | bytes 14745608 | tf_op jit(solution)/shard_map/ppermute | solution.py:17
  19.0 61.0 %collective-permute-start = (bf16[100,24576]{1,0:T(8,128)(2,1)}, bf16[100,24576]{1,0:T(8,128)(2,1)}, u32[]{:S(2)}, u32[]{:S(2)}) collective-permute-start(bf16[100,24576]{1,0:T(8,128)(2,1)} %get-tuple-element.4), channel_id=1, source_target_pairs={{0,1},{1,2},{2,3},{3,4},{4,5},{5,6},{6,7},{7,8},{8,9},{9,10},{10,1... | collective-permute-start | bytes 14745608 | tf_op jit(solution)/shard_map/ppermute | solution.py:15
  90.6 8.9 %copy-start = (bf16[192,24576]{1,0:T(8,128)(2,1)}, bf16[192,24576]{1,0:T(8,128)(2,1)S(1)}, u32[]{:S(2)}) copy-start(bf16[192,24576]{1,0:T(8,128)(2,1)S(1)} %convolution_convert_fusion) | copy-start | bytes 28311556
  100.4 277.1 %reduce-scatter.2.cloned.1.call-start = ((), (), s32[]{:S(2)}) async-start(), calls=%async_computation.1 | async-start | bytes 13369344 | tf_op jit(solution)/shard_map/reduce_scatter | solution.py:42
Sparse Core Ops, SparseCore 0:
  100.5 139.0 all-reduce.2
  244.2 133.1 reduce-scatter.1
where the time goes:
time: 390 us; the launch traced here: 387 us
  waiting for transfers between devices  298 us (76%)
  matrix products  34.9 us (9%)
  other arithmetic  23.7 us (6%)
  between operations  14.1 us (4%)
  local copies, waits for them, and re-layouts  11.6 us (3%)
  starting transfers between devices  4.92 us (1%)
    psum x1, waiting for transfers between devices, on_device(): gram_sum = lax.psum(local_gram, 'tm')  127 us
    reduce_scatter x1, waiting for transfers between devices, on_device(): lax.psum_scatter(jnp.einsum('tc,tr->cr', filtered, sketch, preferred_elem...  112 us
    ppermute x1, waiting for transfers between devices, with_halo(): lax.ppermute(head, axis, [((i + 1) % count, i) for i in range(ends)])  53.4 us
    another operation x3, other arithmetic, on_device(): lower_factor = jnp.linalg.cholesky(gram_sum)  12.4 us
    dot_general x1, matrix products, on_device(): jnp.einsum('tc,tr->cr', filtered, sketch, preferred_element_type=jnp.floa...  11.8 us
    dot_general x1, matrix products, on_device(): jnp.dot(toeplitz, padded, preferred_element_type=jnp.float32)  10.6 us
    another operation x1, other arithmetic, on_device(): lax.linalg.triangular_solve(lower_factor, cross_sums, left_side=False, lo...  9.81 us
    slice x1, local copies, waits for them, and re-layouts, with_halo(): lax.slice_in_dim(cells, cells.shape[dim] - width, cells.shape[dim], axis=...  9.05 us
  transfers between devices with their start and end apart: 4, of which 4 were waited for; matrix products, arithmetic and copies ran while one was open for 10% of the time, Pallas kernels for 0%

commit v1 on v0

v1 whole, which is shorter than its diff:
```python
import functools

import jax
import jax.numpy as jnp
from jax import lax
from jax.experimental import pallas as pl
from jax.experimental.pallas import tpu as pltpu
from jax.sharding import Mesh, PartitionSpec as P

MESH = pl.DeviceIdType.MESH
TEAM = 4
BLOCK = 256


def banded_rows(filter_taps, rows, width, lead):
    taps = filter_taps.shape[0]
    line = jnp.concatenate(
        [jnp.zeros((lead,), filter_taps.dtype), filter_taps, jnp.zeros((width + 1 - lead - taps,), filter_taps.dtype)]
    )
    return jnp.tile(line, rows)[: rows * width].reshape(rows, width)


def team_kernel(
    cut, teams, pad,
    series, band, omega, cross, gram,
    days, filt, om, acc, got, sk,
    local_sem, om_sem, send_sem, recv_sem, hsend, hrecv, ssend, srecv, gsend, grecv,
):
    z, q = lax.axis_index("z"), lax.axis_index("q")
    own = series.shape[0]
    width = filt.shape[1]
    per = width // teams
    span = own * TEAM
    chunks = width // cut
    subs = per // cut
    up, down = lax.rem(z + 1, teams), lax.rem(z + teams - 1, teams)

    barrier = pltpu.get_barrier_semaphore()
    for d in range(1, TEAM):
        pl.semaphore_signal(barrier, inc=1, device_id={"q": lax.rem(q + d, TEAM)}, device_id_type=MESH)
    for other in (up, down):
        pl.semaphore_signal(barrier, inc=1, device_id={"z": other}, device_id_type=MESH)

    def source(k, member):
        start = ((k // subs) * TEAM + member) * per + (k % subs) * cut
        return series.at[:, pl.ds(pl.multiple_of(start, 128), cut)]

    def cols(k):
        return pl.ds(pl.multiple_of(k * cut, 128), cut)

    mine = pl.ds(pl.multiple_of(pad + q * own, 16), own)
    share = pl.ds(pl.multiple_of(q * own, 16), own)

    def local(k):
        return pltpu.make_async_copy(source(k, q), days.at[mine, cols(k)], local_sem.at[k])

    def omega_rows(b):
        rows = pl.ds(pl.multiple_of((b * TEAM + q) * per, 128), per)
        return pltpu.make_async_copy(omega.at[rows, :], om.at[pl.ds(b * per, per), :], om_sem.at[b])

    def give(k, d):
        peer = lax.rem(q + d, TEAM)
        return pltpu.make_async_remote_copy(
            src_ref=source(k, peer), dst_ref=days.at[mine, cols(k)],
            send_sem=send_sem.at[k, d - 1], recv_sem=recv_sem.at[k, d - 1],
            device_id={"q": peer}, device_id_type=MESH,
        )

    def take(k, d):
        origin = lax.rem(q + TEAM - d, TEAM)
        rows = pl.ds(pl.multiple_of(pad + origin * own, 16), own)
        return pltpu.make_async_remote_copy(
            src_ref=days.at[rows, cols(k)], dst_ref=days.at[rows, cols(k)],
            send_sem=send_sem.at[k, d - 1], recv_sem=recv_sem.at[k, d - 1],
            device_id={"q": origin}, device_id_type=MESH,
        )

    def halo_up(k):
        return pltpu.make_async_remote_copy(
            src_ref=days.at[pl.ds(span, pad), cols(k)], dst_ref=days.at[pl.ds(0, pad), cols(k)],
            send_sem=hsend.at[k, 0], recv_sem=hrecv.at[k, 0],
            device_id={"z": up}, device_id_type=MESH,
        )

    def halo_down(k):
        return pltpu.make_async_remote_copy(
            src_ref=days.at[pl.ds(pad, pad), cols(k)], dst_ref=days.at[pl.ds(pad + span, pad), cols(k)],
            send_sem=hsend.at[k, 1], recv_sem=hrecv.at[k, 1],
            device_id={"z": down}, device_id_type=MESH,
        )

    for b in range(teams):
        omega_rows(b).start()
    for k in range(chunks):
        local(k).start()
    pl.semaphore_wait(barrier, TEAM + 1)

    def give_all(k):
        for d in (2, 1, 3):
            give(k, d).start()

    ahead = 2
    for k in range(ahead):
        give_all(k)

    @pl.when(z == 0)
    def _():
        days[:pad, :] = jnp.zeros((pad, width), days.dtype)

    @pl.when(z == teams - 1)
    def _():
        days[pad + span :, :] = jnp.zeros((pad, width), days.dtype)

    acc[...] = jnp.zeros_like(acc)
    for b in range(teams):
        omega_rows(b).wait()

    reach = band.shape[1]

    def step(k, carry):
        @pl.when(k < chunks)
        def _():
            local(k).wait()
            for d in range(1, TEAM):
                take(k, d).wait_recv()

            @pl.when(z < teams - 1)
            def _():
                halo_up(k).start()

            @pl.when(z > 0)
            def _():
                halo_down(k).start()

        @pl.when(k + ahead < chunks)
        def _():
            give_all(k + ahead)

        @pl.when(k >= 1)
        def _():
            p = k - 1

            @pl.when(z > 0)
            def _():
                halo_up(p).wait_recv()

            @pl.when(z < teams - 1)
            def _():
                halo_down(p).wait_recv()

            weights = om[pl.ds(pl.multiple_of(p * cut, 128), cut), :]
            for r in range(span // BLOCK):
                part = jnp.dot(
                    band[...], days[r * BLOCK : r * BLOCK + reach, cols(p)], preferred_element_type=jnp.float32
                ).astype(filt.dtype)
                filt[r * BLOCK : (r + 1) * BLOCK, cols(p)] = part
                acc[r * BLOCK : (r + 1) * BLOCK, :] += jnp.dot(part, weights, preferred_element_type=jnp.float32)

        return carry

    lax.fori_loop(0, chunks + 1, step, 0)

    def part_copy(d):
        peer = lax.rem(q + d, TEAM)
        rows = pl.ds(pl.multiple_of(peer * own, 16), own)
        return pltpu.make_async_remote_copy(
            src_ref=acc.at[rows, :], dst_ref=got.at[d - 1],
            send_sem=ssend.at[d - 1], recv_sem=srecv.at[d - 1],
            device_id={"q": peer}, device_id_type=MESH,
        )

    def done_copy(d):
        return pltpu.make_async_remote_copy(
            src_ref=sk.at[share, :], dst_ref=sk.at[share, :],
            send_sem=gsend.at[d - 1], recv_sem=grecv.at[d - 1],
            device_id={"q": lax.rem(q + d, TEAM)}, device_id_type=MESH,
        )

    def done_take(d):
        origin = lax.rem(q + TEAM - d, TEAM)
        rows = pl.ds(pl.multiple_of(origin * own, 16), own)
        return pltpu.make_async_remote_copy(
            src_ref=sk.at[rows, :], dst_ref=sk.at[rows, :],
            send_sem=gsend.at[d - 1], recv_sem=grecv.at[d - 1],
            device_id={"q": origin}, device_id_type=MESH,
        )

    for d in (2, 1, 3):
        part_copy(d).start()
    for d in range(1, TEAM):
        part_copy(d).wait_recv()
    total = acc[share, :] + got[0] + got[1] + got[2]
    sk[share, :] = total.astype(sk.dtype)
    for d in (2, 1, 3):
        done_copy(d).start()
    for d in range(1, TEAM):
        done_take(d).wait_recv()

    sketch = sk[...]
    turned = sketch.T
    gram[...] = jnp.dot(turned, sketch, preferred_element_type=jnp.float32)

    def product(k, carry):
        cross[:, cols(k)] = jnp.dot(turned, filt[:, cols(k)], preferred_element_type=jnp.float32)
        return carry

    lax.fori_loop(0, chunks, product, 0)

    def drain(k, carry):
        for d in range(1, TEAM):
            give(k, d).wait_send()

        @pl.when(z < teams - 1)
        def _():
            halo_up(k).wait_send()

        @pl.when(z > 0)
        def _():
            halo_down(k).wait_send()

        return carry

    lax.fori_loop(0, chunks, drain, 0)
    for d in range(1, TEAM):
        part_copy(d).wait_send()
        done_copy(d).wait_send()


def on_device(teams, series, filter_taps, test_matrix):
    own, columns = series.shape
    rank = test_matrix.shape[1]
    half_width = (filter_taps.shape[0] - 1) // 2
    pad = -(-half_width // 16) * 16
    span = own * TEAM
    width = columns // TEAM
    per = width // teams
    cut = per // 2 if per % 256 == 0 and per > 512 else per
    chunks = width // cut
    band = banded_rows(filter_taps, BLOCK, BLOCK + 2 * pad, pad - half_width)
    vmem = pl.BlockSpec(memory_space=pltpu.VMEM)
    hbm = pl.BlockSpec(memory_space=pl.ANY)
    dma = pltpu.SemaphoreType.DMA
    flops = 2 * span * width * (BLOCK + 2 * pad + 2 * rank)
    cross, gram = pl.pallas_call(
        functools.partial(team_kernel, cut, teams, pad),
        out_shape=(
            jax.ShapeDtypeStruct((rank, width), jnp.float32),
            jax.ShapeDtypeStruct((rank, rank), jnp.float32),
        ),
        in_specs=[hbm, vmem, hbm],
        out_specs=(vmem, vmem),
        scratch_shapes=[
            pltpu.VMEM((span + 2 * pad, width), jnp.bfloat16),
            pltpu.VMEM((span, width), jnp.bfloat16),
            pltpu.VMEM((width, rank), jnp.bfloat16),
            pltpu.VMEM((span, rank), jnp.float32),
            pltpu.VMEM((TEAM - 1, own, rank), jnp.float32),
            pltpu.VMEM((span, rank), jnp.bfloat16),
            dma((chunks,)),
            dma((teams,)),
            dma((chunks, TEAM - 1)),
            dma((chunks, TEAM - 1)),
            dma((chunks, 2)),
            dma((chunks, 2)),
            dma((TEAM - 1,)),
            dma((TEAM - 1,)),
            dma((TEAM - 1,)),
            dma((TEAM - 1,)),
        ],
        compiler_params=pltpu.CompilerParams(
            collective_id=0, has_side_effects=True, vmem_limit_bytes=56 * 1024 * 1024
        ),
        cost_estimate=pl.CostEstimate(flops=flops, bytes_accessed=2 * own * columns * 3, transcendentals=0),
    )(series, band, test_matrix)
    gram_sum = lax.psum(gram, "z")
    cross_sums = lax.psum_scatter(cross.reshape(rank, teams, per).swapaxes(0, 1), "z", scatter_dimension=0, tiled=False)
    lower_factor = jnp.linalg.cholesky(gram_sum)
    patterns = lax.linalg.triangular_solve(
        lower_factor, cross_sums.T, left_side=False, lower=True, transpose_a=True
    )
    total_days = span * teams
    factor = lower_factor.T * float(total_days) ** (-0.5)
    return (patterns, factor)


def solution(mesh):
    groups, members = mesh.devices.shape
    teams = members // TEAM
    split = Mesh(mesh.devices.reshape(groups, teams, TEAM), ("grp", "z", "q"))
    placed = (P(("z", "q"), "grp"), P(), P())
    return jax.shard_map(
        functools.partial(on_device, teams),
        mesh=split,
        in_specs=placed,
        out_specs=(P(("grp", "z", "q"), None), P("grp", None)),
        check_vma=False,
    )
```

time: 390 us -> 248 us (0.64)
  waiting for transfers between devices: 298 us -> 66.3 us
  Pallas kernels: 0 us -> 128 us
  matrix products: 34.9 us -> 3.41 us
  starting transfers between devices: 4.92 us -> 0.08 us
    pallas_call x0 -> x1, Pallas kernels: none -> 128 us  [on_device(): pl.pallas_call(functools.partial(team_kernel, cut, teams, pad), out_shape...]
    psum x1, waiting for transfers between devices: 127 us -> 29.7 us  [on_device(): gram_sum = lax.psum(gram, 'z')]
    reduce_scatter x1, waiting for transfers between devices: 112 us -> 36.6 us  [on_device(): lax.psum_scatter(cross.reshape(rank, teams, per).swapaxes(0, 1), 'z', sca...]
    ppermute x2 -> x0, waiting for transfers between devices: 58.2 us -> none  [the longest x1 53.4 us: with_halo(): lax.ppermute(head, axis, [((i + 1) % count, i) for i in range(ends)])]
    dot_general x4 -> x0, matrix products: 32.1 us -> none  [the longest x1 11.8 us: on_device(): jnp.einsum('tc,tr->cr', filtered, sketch, preferred_element_type=jnp.floa...]
    slice x1, local copies, waits for them, and re-layouts: 9.05 us -> 0.02 us  [banded_rows(): return jnp.tile(line, rows)[:rows * width].reshape(rows, width)]
    ppermute x2 -> x0, starting transfers between devices: 4.66 us -> none  [the longest x1 2.74 us: with_halo(): lax.ppermute(head, axis, [((i + 1) % count, i) for i in range(ends)])]
    reshape x1 -> x2, local copies, waits for them, and re-layouts: 0.44 us -> 4.91 us  [the longest x1 3.86 us: on_device(): cross.reshape(rank, teams, per).swapaxes(0, 1)]
  transfers between devices with their start and end apart: 4 -> 2, of which waited for: 4 -> 2; matrix products, arithmetic and copies ran while one was open for 10% -> 12% of each run, Pallas kernels for 0% -> 0%
where the time goes in v1:
time: 248 us; the launch traced here: 246 us
  Pallas kernels  128 us (52%)
  waiting for transfers between devices  66.3 us (27%)
  other arithmetic  24.4 us (10%)
  between operations  14.1 us (6%)
  local copies, waits for them, and re-layouts  8.8 us (4%)
  matrix products  3.41 us (1%)
    pallas_call x1, Pallas kernels, on_device(): pl.pallas_call(functools.partial(team_kernel, cut, teams, pad), out_shape...  128 us
    reduce_scatter x1, waiting for transfers between devices, on_device(): lax.psum_scatter(cross.reshape(rank, teams, per).swapaxes(0, 1), 'z', sca...  36.6 us
    psum x1, waiting for transfers between devices, on_device(): gram_sum = lax.psum(gram, 'z')  29.7 us
    another operation x3, other arithmetic, on_device(): lower_factor = jnp.linalg.cholesky(gram_sum)  12.4 us
    another operation x1, other arithmetic, on_device(): lax.linalg.triangular_solve(lower_factor, cross_sums.T, left_side=False,...  9.81 us
  transfers between devices with their start and end apart: 2, of which 2 were waited for; matrix products, arithmetic and copies ran while one was open for 12% of the time, Pallas kernels for 0%

profile of v1, /device:TPU:8, one launch (start us, length us, event | category | flops | bytes accessed | tf_op | source)
XLA Modules:
  0.0 245.6 jit_solution(1665561194349047027)
XLA Ops:
  7.2 0.0 all-reduce.2.cloned.1.call-start
  7.2 0.7 pad_maximum_fusion
  8.0 0.6 tile.10
  8.6 1.1 reshape.20.band
  9.7 128.4 %shard_map.50 = (f32[128,6144]{1,0:T(8,128)}, f32[128,128]{1,0:T(8,128)}) custom-call(bf16[192,24576]{1,0:T(8,128)(2,1)} %series.1, bf16[256,480]{1,0:T(8,128)(2,1)} %reshape.20.band, bf16[24576,128]{1,0:T(8,128)(2,1)} %omega.1), custom_call_target="tpu_custom_call" | custom-call | flops 6945767424 | bytes 28311552 | tf_op jit(solution)/shard_map/pallas_call | solution.py:244
  138.1 1.6 copy.12
  139.7 0.0 all-reduce.2.cloned.1.call-update
  139.7 0.0 reduce-scatter.2.cloned.1.call-start
  139.8 3.9 %copy.17 = f32[16,4,8,1536]{3,2,0,1:T(8,128)} copy(f32[16,4,8,1536]{3,2,1,0:T(8,128)} %bitcast.22) | data formatting | bytes 6291456 | tf_op jit(solution)/shard_map/reshape | solution.py:276
  143.6 0.0 reduce-scatter.2.cloned.1.call-update
  143.6 29.7 %all-reduce.2.cloned.1.call-done = f32[128,128]{0,1:T(8,128)} async-done(((f32[128,128]{0,1:T(8,128)}), f32[128,128]{0,1:T(8,128)}) %all-reduce.2.cloned.1.call-update) | async-done | bytes 65552 | tf_op jit(solution)/shard_map/psum | solution.py:275
  173.3 0.9 copy.13
  174.3 0.9 fusion.3
  175.1 11.7 %cholesky.16 = f32[128,128]{1,0:T(8,128)S(1)} custom-call(f32[128,128]{1,0:T(8,128)S(1)} %fusion.3), custom_call_target="Cholesky" | custom-call | tf_op jit(solution)/shard_map/jit(cholesky)/cholesky | solution.py:277
  186.9 0.6 compare_reduce_fusion
  187.5 0.7 multiply_bitcast_fusion
  188.2 0.7 copy.14
  188.9 9.8 %custom-call.6 = f32[1,128,128]{1,2,0:T(8,128)S(1)} custom-call(f32[1,128,128]{2,1,0:T(8,128)S(1)} %get-tuple-element.13), custom_call_target="InvertDiagBlocksLowerTriangular" | custom-call | tf_op jit(solution)/shard_map/triangular_solve | solution.py:278
  198.7 36.6 %reduce-scatter.2.cloned.1.call-done = f32[1,128,1536]{2,1,0:T(8,128)} async-done(((f32[4,128,1536]{2,1,0:T(8,128)}), f32[1,128,1536]{2,1,0:T(8,128)}) %reduce-scatter.2.cloned.1.call-update) | async-done | bytes 786448 | tf_op jit(solution)/shard_map/reduce_scatter | solution.py:276
  235.3 3.4 %fusion = f32[1536,128]{1,0:T(8,128)} fusion(f32[1,128,1536]{2,1,0:T(8,128)} %reduce-scatter.2.cloned.1.call-done, f32[1,128,128]{1,2,0:T(8,128)S(1)} %custom-call.6), kind=kOutput, calls=%fused_computation.1 | convolution fusion | flops 301989888 | bytes 1638400 | tf_op jit(solution)/shard_map/triangular_solve | solution.py:278
  (5 shorter events, 0.1 us)
Async XLA Ops:
  7.2 166.2 %all-reduce.2.cloned.1.call-start = ((), (), s32[]{:S(2)}) async-start(), calls=%async_computation.2 | async-start | bytes 131072 | tf_op jit(solution)/shard_map/psum | solution.py:275
  139.7 95.6 %reduce-scatter.2.cloned.1.call-start = ((), (), s32[]{:S(2)}) async-start(), calls=%async_computation.1 | async-start | bytes 3932160 | tf_op jit(solution)/shard_map/reduce_scatter | solution.py:276
Sparse Core Ops, SparseCore 0:
  139.8 33.4 all-reduce.1
  175.7 59.5 reduce-scatter.1

commit v2 on v1

--- a/solution.py
+++ b/solution.py
@@ -22,9 +22,9 @@
 
 def team_kernel(
     cut, teams, pad,
-    series, band, omega, cross, gram,
-    days, filt, om, acc, got, sk,
-    local_sem, om_sem, send_sem, recv_sem, hsend, hrecv, ssend, srecv, gsend, grecv,
+    series, band, omega, patterns, factor,
+    days, filt, om, acc, got, sk, grams, tri, cross, landed,
+    local_sem, om_sem, send_sem, recv_sem, hsend, hrecv, ssend, srecv, gsend, grecv, msend, mrecv, rsend, rrecv,
 ):
     z, q = lax.axis_index("z"), lax.axis_index("q")
     own = series.shape[0]
@@ -38,8 +38,8 @@
     barrier = pltpu.get_barrier_semaphore()
     for d in range(1, TEAM):
         pl.semaphore_signal(barrier, inc=1, device_id={"q": lax.rem(q + d, TEAM)}, device_id_type=MESH)
-    for other in (up, down):
-        pl.semaphore_signal(barrier, inc=1, device_id={"z": other}, device_id_type=MESH)
+    for d in range(1, teams):
+        pl.semaphore_signal(barrier, inc=1, device_id={"z": lax.rem(z + d, teams)}, device_id_type=MESH)
 
     def source(k, member):
         start = ((k // subs) * TEAM + member) * per + (k % subs) * cut
@@ -93,7 +93,7 @@
         omega_rows(b).start()
     for k in range(chunks):
         local(k).start()
-    pl.semaphore_wait(barrier, TEAM + 1)
+    pl.semaphore_wait(barrier, TEAM + teams - 2)
 
     def give_all(k):
         for d in (2, 1, 3):
@@ -198,13 +198,118 @@
 
     sketch = sk[...]
     turned = sketch.T
-    gram[...] = jnp.dot(turned, sketch, preferred_element_type=jnp.float32)
-
-    def product(k, carry):
-        cross[:, cols(k)] = jnp.dot(turned, filt[:, cols(k)], preferred_element_type=jnp.float32)
+    rank = sketch.shape[1]
+    grams[0] = jnp.dot(turned, sketch, preferred_element_type=jnp.float32)
+
+    def gram_copy(d):
+        return pltpu.make_async_remote_copy(
+            src_ref=grams.at[0], dst_ref=grams.at[d],
+            send_sem=msend.at[d - 1], recv_sem=mrecv.at[d - 1],
+            device_id={"z": lax.rem(z + d, teams)}, device_id_type=MESH,
+        )
+
+    for d in range(1, teams):
+        gram_copy(d).start()
+
+    def sum_right(c):
+        return pltpu.make_async_remote_copy(
+            src_ref=cross.at[c], dst_ref=landed.at[c],
+            send_sem=rsend.at[c], recv_sem=rrecv.at[c],
+            device_id={"z": up}, device_id_type=MESH,
+        )
+
+    def sum_left(c):
+        slot = jnp.where(c == down, teams, c)
+        return pltpu.make_async_remote_copy(
+            src_ref=cross.at[c], dst_ref=landed.at[slot],
+            send_sem=rsend.at[c], recv_sem=rrecv.at[slot],
+            device_id={"z": down}, device_id_type=MESH,
+        )
+
+    def arrived(slot):
+        return pltpu.make_async_remote_copy(
+            src_ref=landed.at[slot], dst_ref=landed.at[slot],
+            send_sem=rsend.at[0], recv_sem=rrecv.at[slot],
+            device_id={"z": up}, device_id_type=MESH,
+        )
+
+    order = []
+    for i in range((teams + 1) // 2):
+        order += [teams - 1 - i] + ([i] if i != teams - 1 - i else [])
+    for c in order:
+        for s in range(subs):
+            k = c * subs + s
+            cross[c, :, s * cut : (s + 1) * cut] = jnp.dot(
+                turned, filt[:, k * cut : (k + 1) * cut], preferred_element_type=jnp.float32
+            )
+        if c > 0:
+            @pl.when(z == 0)
+            def _():
+                sum_right(c).start()
+        if c < teams - 1:
+            @pl.when(z == teams - 1)
+            def _():
+                sum_left(c).start()
+
+    for d in range(1, teams):
+        gram_copy(d).wait_recv()
+    whole = grams[0]
+    for d in range(1, teams):
+        whole = whole + grams[d]
+    row = lax.broadcasted_iota(jnp.int32, (rank, rank), 0)
+    col = lax.broadcasted_iota(jnp.int32, (rank, rank), 1)
+    tri[:, :rank] = whole
+    tri[:, rank:] = jnp.where(row == col, 1.0, 0.0).astype(jnp.float32)
+    lane = lax.broadcasted_iota(jnp.int32, (1, rank), 1)
+    eye = row == col
+    below = lax.broadcasted_iota(jnp.int32, (rank, 1), 0)
+
+    def eliminate(j, carry):
+        line = tri[pl.ds(j, 1), :]
+        pivot = jnp.sum(jnp.where(lane == j, line[:, :rank], 0.0), axis=1, keepdims=True)
+        line = line * (1.0 / jnp.sqrt(pivot))
+        mult = jnp.sum(jnp.where(eye, line[:, :rank], 0.0), axis=1, keepdims=True)
+        tri[...] = tri[...] - jnp.where(below > j, mult, 0.0) * line
+        tri[pl.ds(j, 1), :] = line
         return carry
 
-    lax.fori_loop(0, chunks, product, 0)
+    piece = rank // teams
+    for i in range(teams):
+        lax.fori_loop(i * piece, (i + 1) * piece, eliminate, 0)
+        if 0 < teams - 1 - i:
+            c = teams - 1 - i
+            @pl.when((z > 0) & (z < c))
+            def _():
+                arrived(c).wait_recv()
+                cross[c] = cross[c] + landed[c]
+                sum_right(c).start()
+        if i < teams - 1:
+            @pl.when((z < teams - 1) & (z > i))
+            def _():
+                arrived(i).wait_recv()
+                cross[i] = cross[i] + landed[i]
+                sum_left(i).start()
+
+    upper = jnp.where(row <= col, tri[:, :rank], 0.0)
+    factor[...] = upper * float(span * teams) ** (-0.5)
+    inverse = jnp.where(row >= col, tri[:, rank:], 0.0)
+
+    @pl.when(z > 0)
+    def _():
+        arrived(z).wait_recv()
+        cross[z] = cross[z] + landed[z]
+
+    @pl.when(z < teams - 1)
+    def _():
+        arrived(teams).wait_recv()
+        cross[z] = cross[z] + landed[teams]
+
+    for s in range(subs):
+        solved = jnp.dot(
+            inverse, cross[z, :, s * cut : (s + 1) * cut],
+            preferred_element_type=jnp.float32, precision=lax.Precision.HIGHEST,
+        )
+        patterns[s * cut : (s + 1) * cut, :] = solved.T
 
     def drain(k, carry):
         for d in range(1, TEAM):
@@ -224,6 +329,12 @@
     for d in range(1, TEAM):
         part_copy(d).wait_send()
         done_copy(d).wait_send()
+    for d in range(1, teams):
+        gram_copy(d).wait_send()
+    for c in range(teams):
+        @pl.when(c != z)
+        def _():
+            sum_right(c).wait_send()
 
 
 def on_device(teams, series, filter_taps, test_matrix):
@@ -241,10 +352,10 @@
     hbm = pl.BlockSpec(memory_space=pl.ANY)
     dma = pltpu.SemaphoreType.DMA
     flops = 2 * span * width * (BLOCK + 2 * pad + 2 * rank)
-    cross, gram = pl.pallas_call(
+    return pl.pallas_call(
         functools.partial(team_kernel, cut, teams, pad),
         out_shape=(
-            jax.ShapeDtypeStruct((rank, width), jnp.float32),
+            jax.ShapeDtypeStruct((per, rank), jnp.float32),
             jax.ShapeDtypeStruct((rank, rank), jnp.float32),
         ),
         in_specs=[hbm, vmem, hbm],
@@ -256,6 +367,10 @@
             pltpu.VMEM((span, rank), jnp.float32),
             pltpu.VMEM((TEAM - 1, own, rank), jnp.float32),
             pltpu.VMEM((span, rank), jnp.bfloat16),
+            pltpu.VMEM((teams, rank, rank), jnp.float32),
+            pltpu.VMEM((rank, 2 * rank), jnp.float32),
+            pltpu.VMEM((teams, rank, per), jnp.float32),
+            pltpu.VMEM((teams + 1, rank, per), jnp.float32),
             dma((chunks,)),
             dma((teams,)),
             dma((chunks, TEAM - 1)),
@@ -266,21 +381,16 @@
             dma((TEAM - 1,)),
             dma((TEAM - 1,)),
             dma((TEAM - 1,)),
+            dma((teams - 1,)),
+            dma((teams - 1,)),
+            dma((teams,)),
+            dma((teams + 1,)),
         ],
         compiler_params=pltpu.CompilerParams(
             collective_id=0, has_side_effects=True, vmem_limit_bytes=56 * 1024 * 1024
         ),
         cost_estimate=pl.CostEstimate(flops=flops, bytes_accessed=2 * own * columns * 3, transcendentals=0),
     )(series, band, test_matrix)
-    gram_sum = lax.psum(gram, "z")
-    cross_sums = lax.psum_scatter(cross.reshape(rank, teams, per).swapaxes(0, 1), "z", scatter_dimension=0, tiled=False)
-    lower_factor = jnp.linalg.cholesky(gram_sum)
-    patterns = lax.linalg.triangular_solve(
-        lower_factor, cross_sums.T, left_side=False, lower=True, transpose_a=True
-    )
-    total_days = span * teams
-    factor = lower_factor.T * float(total_days) ** (-0.5)
-    return (patterns, factor)
 
 
 def solution(mesh):

time: 248 us -> 214 us (0.86)
  Pallas kernels: 128 us -> 205 us
  waiting for transfers between devices: 66.3 us -> 0 us
  other arithmetic: 24.4 us -> 0.73 us
  between operations: 14.1 us -> 0.67 us
  local copies, waits for them, and re-layouts: 8.8 us -> 5.26 us
  matrix products: 3.41 us -> 0 us
    pallas_call x1, Pallas kernels: 128 us -> 205 us  [on_device(): pl.pallas_call(functools.partial(team_kernel, cut, teams, pad), out_shape...]
    reduce_scatter x1 -> x0, waiting for transfers between devices: 36.6 us -> none  [on_device(): lax.psum_scatter(cross.reshape(rank, teams, per).swapaxes(0, 1), 'z', sca...]
    psum x1 -> x0, waiting for transfers between devices: 29.7 us -> none  [on_device(): gram_sum = lax.psum(gram, 'z')]
    another operation x4 -> x0, other arithmetic: 22.2 us -> none  [the longest x3 12.4 us: on_device(): lower_factor = jnp.linalg.cholesky(gram_sum)]
    reshape x1 -> x0, local copies, waits for them, and re-layouts: 3.86 us -> none  [on_device(): cross.reshape(rank, teams, per).swapaxes(0, 1)]
    another operation x1 -> x0, matrix products: 3.41 us -> none  [on_device(): lax.linalg.triangular_solve(lower_factor, cross_sums.T, left_side=False,...]
    unnamed x1 -> x2, local copies, waits for them, and re-layouts: 0.73 us -> 3.54 us
  transfers between devices with their start and end apart: 2 -> 0, of which waited for: 2 -> 0; matrix products, arithmetic and copies ran while one was open for 12% -> 0% of each run, Pallas kernels for 0% -> 0%
where the time goes in v2:
time: 214 us; the launch traced here: 211 us
  Pallas kernels  205 us (96%)
  local copies, waits for them, and re-layouts  5.26 us (2%)
    pallas_call x1, Pallas kernels, on_device(): pl.pallas_call(functools.partial(team_kernel, cut, teams, pad), out_shape...  205 us

profile of v2, /device:TPU:8, one launch (start us, length us, event | category | flops | bytes accessed | tf_op | source)
XLA Modules:
  0.0 211.5 jit_solution(5216203018912900640)
XLA Ops:
  0.7 0.7 pad_maximum_fusion
  1.4 0.6 tile.10
  2.1 1.1 reshape.8.band
  3.1 204.8 %shard_map.50 = (f32[1536,128]{1,0:T(8,128)}, f32[128,128]{1,0:T(8,128)}) custom-call(bf16[192,24576]{1,0:T(8,128)(2,1)} %series.1, bf16[256,480]{1,0:T(8,128)(2,1)} %reshape.8.band, bf16[24576,128]{1,0:T(8,128)(2,1)} %omega.1), custom_call_target="tpu_custom_call" | custom-call | flops 6945767424 | bytes 28311552 | tf_op jit(solution)/shard_map/pallas_call | solution.py:355
  207.9 2.1 copy.7
  210.0 1.5 copy.8
  (4 shorter events, 0.0 us)

commit v3 on v2

--- a/solution.py
+++ b/solution.py
@@ -10,6 +10,9 @@
 MESH = pl.DeviceIdType.MESH
 TEAM = 4
 BLOCK = 256
+REACH = 86.0
+TINY = 1e-30
+SIDE = 16
 
 
 def banded_rows(filter_taps, rows, width, lead):
@@ -23,7 +26,7 @@
 def team_kernel(
     cut, teams, pad,
     series, band, omega, patterns, factor,
-    days, filt, om, acc, got, sk, grams, tri, cross, landed,
+    days, filt, om, acc, got, sk, grams, tri, cross, wire, landed,
     local_sem, om_sem, send_sem, recv_sem, hsend, hrecv, ssend, srecv, gsend, grecv, msend, mrecv, rsend, rrecv,
 ):
     z, q = lax.axis_index("z"), lax.axis_index("q")
@@ -213,7 +216,7 @@
 
     def sum_right(c):
         return pltpu.make_async_remote_copy(
-            src_ref=cross.at[c], dst_ref=landed.at[c],
+            src_ref=wire.at[c], dst_ref=landed.at[c],
             send_sem=rsend.at[c], recv_sem=rrecv.at[c],
             device_id={"z": up}, device_id_type=MESH,
         )
@@ -221,7 +224,7 @@
     def sum_left(c):
         slot = jnp.where(c == down, teams, c)
         return pltpu.make_async_remote_copy(
-            src_ref=cross.at[c], dst_ref=landed.at[slot],
+            src_ref=wire.at[c], dst_ref=landed.at[slot],
             send_sem=rsend.at[c], recv_sem=rrecv.at[slot],
             device_id={"z": down}, device_id_type=MESH,
         )
@@ -242,15 +245,54 @@
             cross[c, :, s * cut : (s + 1) * cut] = jnp.dot(
                 turned, filt[:, k * cut : (k + 1) * cut], preferred_element_type=jnp.float32
             )
+
+    def encode(c):
+        for s in range(subs):
+            here = slice(s * cut, (s + 1) * cut)
+            value = cross[c, :, here]
+            size = jnp.abs(value)
+            scale = jnp.maximum(jnp.max(size, axis=0, keepdims=True), TINY).astype(wire.dtype)
+            code = jnp.exp(size * (2 * REACH / scale.astype(jnp.float32)) - REACH)
+            wire[c, :rank, here] = jnp.where(value < 0, -code, code).astype(wire.dtype)
+            wire[c, rank:, here] = jnp.broadcast_to(scale.astype(jnp.float32), (SIDE, cut)).astype(wire.dtype)
+
+    def absorb(c, slot):
+        for s in range(subs):
+            here = slice(s * cut, (s + 1) * cut)
+            code = landed[slot, :rank, here].astype(jnp.float32)
+            scale = landed[slot, rank:, here].astype(jnp.float32)[:1]
+            size = (jnp.log(jnp.abs(code)) + REACH) * (scale * (0.5 / REACH))
+            cross[c, :, here] = cross[c, :, here] + jnp.where(code < 0, -size, size)
+
+    def pass_right(c, first):
+        if not first:
+            arrived(c).wait_recv()
+            absorb(c, c)
+        if c < teams - 1:
+            sum_right(c + 1).wait_send()
+        encode(c)
+        sum_right(c).start()
+
+    def pass_left(c, first):
+        if not first:
+            arrived(c).wait_recv()
+            absorb(c, c)
         if c > 0:
+            sum_left(c - 1).wait_send()
+        encode(c)
+        sum_left(c).start()
+
+    def ends(i):
+        if i < teams - 1:
             @pl.when(z == 0)
             def _():
-                sum_right(c).start()
-        if c < teams - 1:
+                pass_right(teams - 1 - i, True)
+
             @pl.when(z == teams - 1)
             def _():
-                sum_left(c).start()
-
+                pass_left(i, True)
+
+    ends(0)
     for d in range(1, teams):
         gram_copy(d).wait_recv()
     whole = grams[0]
@@ -275,20 +317,18 @@
 
     piece = rank // teams
     for i in range(teams):
+        if i > 0:
+            ends(i)
         lax.fori_loop(i * piece, (i + 1) * piece, eliminate, 0)
-        if 0 < teams - 1 - i:
-            c = teams - 1 - i
+        c = teams - 1 - i
+        if c > 0:
             @pl.when((z > 0) & (z < c))
             def _():
-                arrived(c).wait_recv()
-                cross[c] = cross[c] + landed[c]
-                sum_right(c).start()
+                pass_right(c, False)
         if i < teams - 1:
             @pl.when((z < teams - 1) & (z > i))
             def _():
-                arrived(i).wait_recv()
-                cross[i] = cross[i] + landed[i]
-                sum_left(i).start()
+                pass_left(i, False)
 
     upper = jnp.where(row <= col, tri[:, :rank], 0.0)
     factor[...] = upper * float(span * teams) ** (-0.5)
@@ -297,12 +337,12 @@
     @pl.when(z > 0)
     def _():
         arrived(z).wait_recv()
-        cross[z] = cross[z] + landed[z]
+        absorb(z, z)
 
     @pl.when(z < teams - 1)
     def _():
         arrived(teams).wait_recv()
-        cross[z] = cross[z] + landed[teams]
+        absorb(z, teams)
 
     for s in range(subs):
         solved = jnp.dot(
@@ -331,10 +371,14 @@
         done_copy(d).wait_send()
     for d in range(1, teams):
         gram_copy(d).wait_send()
-    for c in range(teams):
-        @pl.when(c != z)
-        def _():
-            sum_right(c).wait_send()
+
+    @pl.when(z < teams - 1)
+    def _():
+        sum_right(z + 1).wait_send()
+
+    @pl.when(z > 0)
+    def _():
+        sum_left(z - 1).wait_send()
 
 
 def on_device(teams, series, filter_taps, test_matrix):
@@ -370,7 +414,8 @@
             pltpu.VMEM((teams, rank, rank), jnp.float32),
             pltpu.VMEM((rank, 2 * rank), jnp.float32),
             pltpu.VMEM((teams, rank, per), jnp.float32),
-            pltpu.VMEM((teams + 1, rank, per), jnp.float32),
+            pltpu.VMEM((teams, rank + SIDE, per), jnp.bfloat16),
+            pltpu.VMEM((teams + 1, rank + SIDE, per), jnp.bfloat16),
             dma((chunks,)),
             dma((teams,)),
             dma((chunks, TEAM - 1)),

time: 214 us -> 193 us (0.902); the launches traced: 211 us -> 193 us
  Pallas kernels: 205 us -> 186 us
    pallas_call x1, Pallas kernels: 205 us -> 186 us  [on_device(): pl.pallas_call(functools.partial(team_kernel, cut, teams, pad), out_shape...]
where the time goes in v3:
time: 193 us
  Pallas kernels  186 us (96%)
  local copies, waits for them, and re-layouts  5.26 us (3%)
    pallas_call x1, Pallas kernels, on_device(): pl.pallas_call(functools.partial(team_kernel, cut, teams, pad), out_shape...  186 us

profile of v3, /device:TPU:8, one launch (start us, length us, event | category | flops | bytes accessed | tf_op | source)
XLA Modules:
  0.0 192.8 jit_solution(18148337857067399128)
XLA Ops:
  0.7 0.7 pad_maximum_fusion
  1.4 0.6 tile.10
  2.1 1.1 reshape.8.band
  3.1 186.1 %shard_map.50 = (f32[1536,128]{1,0:T(8,128)}, f32[128,128]{1,0:T(8,128)}) custom-call(bf16[192,24576]{1,0:T(8,128)(2,1)} %series.1, bf16[256,480]{1,0:T(8,128)(2,1)} %reshape.8.band, bf16[24576,128]{1,0:T(8,128)(2,1)} %omega.1), custom_call_target="tpu_custom_call" | custom-call | flops 6945767424 | bytes 28311552 | tf_op jit(solution)/shard_map/pallas_call | solution.py:399
  189.3 2.1 %copy.7 = f32[1536,128]{1,0:T(8,128)} copy(f32[1536,128]{1,0:T(8,128)} %get-tuple-element.4) | data formatting | bytes 1572864
  191.3 1.5 copy.8
  (4 shorter events, 0.0 us)
